TPU v7x, 256 devices: a whole 4x4x8 slice. The times are simulated.
256 devices in a mesh: pts: 64 (over x, z, core), cam: 4 (over y).
Axes of the slice: x: 4, y: 4, z: 8, core: 2. Of those that a mesh axis runs over, the one named last changes fastest.
Arguments:
- jac_cam: float32 [4, 2, 6, 524288], P(None, None, None, ('pts', 'cam')), may hold values from -0.6 to 0.6
- jac_pt: float32 [4, 2, 3, 524288], P(None, None, None, ('pts', 'cam')), may hold values from -3 to 3
- resid: float32 [4, 2, 524288], P(None, None, ('pts', 'cam')), may hold values from -6 to 6
- point_damping: float32 [524288], P(('pts', 'cam')), may hold values from 0.5 to 4
- cluster: int32 [524288, 1], P(('pts', 'cam')), may hold values from 0 to 63; in each aligned block of 2048 rows (0 to 2047, 2048 to 4095, ...) at most 64 rows name the same one
- cam_local: int32 [524288, 4], P(('pts', 'cam')), may hold values from 0 to 511, all different within a row
- direction: float32 [6, 32768], P(None, ('pts', 'cam')), may hold values from -6 to 6
- cam_damping: float32 [32768], P(('pts', 'cam')), may hold values from 0.5 to 4
Outputs:
- grad_reduced: float32 [6, 32768], P(None, ('pts', 'cam'))
- schur_dir: float32 [6, 32768], P(None, ('pts', 'cam'))
Inputs may be any that keep to these rules, and one draw needn't show every extreme that they name: In the block of 2048 points of one device no cluster is seen by more than 64 points, a bound that some block reaches. `cam_local`: the 4 cameras of one point are distinct.
All inputs are finite; a program needn't handle non-finite values.
Results may differ from a plain program's by a relative error of at most 0.00011.
Values sent between devices are 32-bit elements; how exact they have to be, the bound alone decides.
A program may use at most 64 MiB of HBM per device.

v0:
```python
import jax
import jax.numpy as jnp
from jax import lax
from jax.experimental import pallas as pl
from jax.experimental.pallas import tpu as pltpu
from jax.sharding import PartitionSpec as P

MESH = pl.DeviceIdType.MESH
F32 = jnp.float32
BF16 = jnp.bfloat16
NX, NY, NZ, NC = 4, 4, 8, 2
POINTS = 2048
CHUNK = 256
ROWS = 176
TRACK = 4
TRANSPOSED = (((1,), (1,)), ((), ()))


def split(value):
    high = value.astype(BF16)
    low = (value - high.astype(F32)).astype(BF16)
    return high, low


def kernel(
    jc_ref, jp_ref, rs_ref, damp_ref, clu_ref, loc_ref, dir_ref, cdamp_ref,
    og_ref, os_ref,
    bt, rt, srow, lhs, sb, lb, db, vb, ohb, tt,
    zb, p0, qa, qb, ra, rb,
    gbuf, sbuf, in1g, in1s, r1ag, r1bg, r1as, r1bs, in2ag, in2bg, in2as, in2bs,
    r2ag, r2bg, r2as, r2bs, in3ag, in3bg, in3as, in3bs, r3g, r3s, r4g, r4s, in4g, in4s,
    send, recv,
):
    me = lax.axis_index("pts")
    y = lax.axis_index("cam")
    core = lax.rem(me, NC)
    z = lax.rem(lax.div(me, NC), NZ)
    x = lax.div(me, NC * NZ)

    def device(xx, yy, zz, cc):
        return {"pts": (xx * NZ + zz) * NC + cc, "cam": yy}

    def step(at, d, size):
        return lax.rem(at + d, size)

    def rows(ref, start, count):
        return ref.at[pl.ds(pl.multiple_of(start, 8), count), :]

    def copy(src, dst, sem, dev):
        return pltpu.make_async_remote_copy(
            src_ref=src, dst_ref=dst, send_sem=send.at[sem], recv_sem=recv.at[sem],
            device_id=dev, device_id_type=MESH,
        )

    def gather_z():
        return [
            copy(dir_ref, rows(zb, z * 8, 6), d - 1, device(x, y, step(z, d, NZ), core))
            for d in range(1, NZ)
        ]

    def gather_first():
        return [
            copy(rows(p0, 0, 24), rows(qa, x * 24, 24), 6 + d, device(step(x, d, NX), y, z, core))
            for d in range(1, NX)
        ] + [
            copy(rows(p0, 24, 24), rows(qb, y * 24, 24), 9 + d, device(x, step(y, d, NY), z, core))
            for d in range(1, NY)
        ]

    def gather_second():
        return [
            copy(qa, rows(ra, (core * NY + y) * 96, 96), 12 + d,
                 device(x, step(y, d, NY), z, core))
            for d in range(1, NY)
        ] + [
            copy(qb, rows(rb, (x * NC + core) * 96, 96), 15 + d,
                 device(step(x, d, NX), y, z, core))
            for d in range(1, NX)
        ]

    def gather_core():
        other = device(x, y, z, 1 - core)
        mine = rows(ra, core * 384, 384)
        out = [copy(mine, mine, 19, other)]
        for xx in range(NX):
            part = rows(rb, (xx * NC + core) * 96, 96)
            out.append(copy(part, part, 20 + xx, other))
        return out

    def sum_core(base, dense, in1, xx):
        return copy(
            rows(dense, (xx * NC + 1 - core) * 192, 192), rows(in1, xx * 192, 192),
            base + xx, device(x, y, z, 1 - core),
        )

    def sum_first(base, r1a, r1b, in2a, in2b):
        return [
            copy(rows(r1a, step(x, d, NX) * 96, 96), rows(in2a, x * 96, 96), base + 3 + d,
                 device(step(x, d, NX), y, z, core))
            for d in range(1, NX)
        ] + [
            copy(rows(r1b, step(y, d, NY) * 96, 96), rows(in2b, y * 96, 96), base + 6 + d,
                 device(x, step(y, d, NY), z, core))
            for d in range(1, NY)
        ]

    def sum_second(base, r2a, r2b, in3a, in3b):
        return [
            copy(rows(r2a, step(y, d, NY) * 24, 24), rows(in3a, y * 24, 24), base + 9 + d,
                 device(x, step(y, d, NY), z, core))
            for d in range(1, NY)
        ] + [
            copy(rows(r2b, step(x, d, NX) * 24, 24), rows(in3b, x * 24, 24), base + 12 + d,
                 device(step(x, d, NX), y, z, core))
            for d in range(1, NX)
        ]

    def sum_z(base, r4, in4):
        return [
            copy(rows(r4, step(z, d, NZ) * 8, 8), rows(in4, z * 8, 8), base + 15 + d,
                 device(x, y, step(z, d, NZ), core))
            for d in range(1, NZ)
        ]

    def start(copies):
        for item in copies:
            item.start()

    def wait(copies):
        for item in copies:
            item.wait()

    def fold_core(dense, in1, r1a, r1b):
        for xx in range(NX):
            total = (
                dense[pl.ds(pl.multiple_of((xx * NC + core) * 192, 8), 192), :]
                + in1[pl.ds(xx * 192, 192), :]
            )
            for yy in range(NY):
                r1a[pl.ds(xx * 96 + yy * 24, 24), :] = total[yy * 48:yy * 48 + 24]
                r1b[pl.ds(yy * 96 + xx * 24, 24), :] = total[yy * 48 + 24:yy * 48 + 48]

    def fold(own, arrived, at, size, count):
        total = own[pl.ds(pl.multiple_of(at * count, 8), count), :]
        for d in range(1, size):
            total += arrived[pl.ds(pl.multiple_of(step(at, d, size) * count, 8), count), :]
        return total

    barrier = pltpu.get_barrier_semaphore()
    peers = [device(step(x, d, NX), y, z, core) for d in range(1, NX)]
    peers += [device(x, step(y, d, NY), z, core) for d in range(1, NY)]
    peers += [device(x, y, step(z, d, NZ), core) for d in range(1, NZ)]
    peers += [device(x, y, z, 1 - core)]
    for dev in peers:
        pl.semaphore_signal(barrier, inc=1, device_id=dev, device_id_type=MESH)

    for kk in range(8):
        for b in range(POINTS // 128):
            bt[b, pl.ds(kk, 3, stride=8), :] = jp_ref[kk, :, pl.ds(b * 128, 128)]
    for kk in range(TRACK):
        rt[pl.ds(2 * kk, 2), :] = rs_ref[kk]
    tt[...] = jnp.zeros_like(tt)
    r4g[...] = jnp.zeros_like(r4g)
    r4s[...] = jnp.zeros_like(r4s)

    pl.semaphore_wait(barrier, len(peers))
    start(gather_z())

    lane = lax.broadcasted_iota(jnp.int32, (CHUNK, CHUNK + 128), 1)
    before = (
        (lax.broadcasted_iota(jnp.int32, (CHUNK, CHUNK + 128), 0) < lane) | (lane >= CHUNK)
    ).astype(F32).astype(BF16)

    def eliminate(b, seen):
        here = pl.ds(pl.multiple_of(b * CHUNK, CHUNK), CHUNK)
        cluster = clu_ref[:, here]
        member = (
            lax.broadcasted_iota(jnp.int32, (64, CHUNK), 0) == jnp.broadcast_to(cluster, (64, CHUNK))
        ).astype(F32)
        counts = jnp.dot(member.astype(BF16), before, preferred_element_type=F32)
        ahead = counts[:, :CHUNK] + jnp.concatenate([seen, seen], axis=1)
        position = jnp.sum(member * ahead, axis=0, keepdims=True)
        slot = jnp.bitwise_and(cluster, 15) * 64 + position.astype(jnp.int32)
        srow[:, here] = slot
        quarter = lax.shift_right_logical(cluster, 4)

        b0, b1, b2 = (
            jnp.concatenate([bt[2 * b + i, pl.ds(8 * j, 8), :] for i in range(2)], axis=1)
            for j in range(3)
        )
        res = rt[:, here]

        def total(value):
            return jnp.sum(value, axis=0, keepdims=True)

        damp = damp_ref[:, here]
        n00, n10, n20 = total(b0 * b0) + damp, total(b1 * b0), total(b2 * b0)
        n11, n21, n22 = total(b1 * b1) + damp, total(b2 * b1), total(b2 * b2) + damp
        q0, q1, q2 = total(b0 * res), total(b1 * res), total(b2 * res)
        ia = 1.0 / jnp.sqrt(n00)
        ba, ca = n10 * ia, n20 * ia
        ib = 1.0 / jnp.sqrt(n11 - ba * ba)
        cb = (n21 - ca * ba) * ib
        ic = 1.0 / jnp.sqrt(n22 - ca * ca - cb * cb)
        c0 = b0 * ia
        c1 = (b1 - ba * c0) * ib
        c2 = (b2 - ca * c0 - cb * c1) * ic
        s0 = q0 * ia
        s1 = (q1 - ba * s0) * ib
        s2 = (q2 - ca * s0 - cb * s1) * ic
        rest = res - (c0 * s0 + c1 * s1 + c2 * s2)

        masks = [
            jnp.broadcast_to((quarter == f).astype(F32), (16, CHUNK)).astype(BF16)
            for f in range(NX)
        ]

        def put(base, value):
            for f in range(NX):
                lhs[pl.ds(f * ROWS + base, 16), here] = value * masks[f]

        for pair in range(4):
            parts = []
            for kk in (2 * pair, 2 * pair + 1):
                parts += [jc_ref[kk, :, here], c0[kk:kk + 1], c1[kk:kk + 1]]
            high, low = split(jnp.concatenate(parts, axis=0))
            put(16 * pair, high)
            put(80 + 16 * pair, low)
        high, low = split(jnp.concatenate([c2, rest], axis=0))
        put(64, high)
        put(144, low)
        label = loc_ref[:, here]
        parts = [
            lax.shift_right_logical(label, 7).astype(F32),
            jnp.bitwise_and(label, 127).astype(F32),
            jnp.zeros((8, CHUNK), F32),
        ]
        put(160, jnp.concatenate(parts, axis=0).astype(BF16))
        return seen + counts[:, CHUNK:]

    lax.fori_loop(0, POINTS // CHUNK, eliminate, jnp.zeros((64, 128), F32))

    wait(gather_z())
    zb[pl.ds(pl.multiple_of(z * 8, 8), 6), :] = dir_ref[...]
    for zz in range(NZ):
        p0[pl.ds(zz, 6, stride=8), :] = zb[pl.ds(zz * 8, 6), :]
    start(gather_first())

    half = jnp.where(lax.broadcasted_iota(jnp.int32, (8, 128), 1) >= 64, 4.0, 0.0)
    half = jnp.where(lax.broadcasted_iota(jnp.int32, (8, 128), 0) < 4, half, 0.0)

    def sort(q, carry):
        slots = lax.broadcasted_iota(jnp.int32, (256, POINTS), 0) + q * 256
        place = (slots == jnp.broadcast_to(srow[...], (256, POINTS))).astype(F32).astype(BF16)
        out = lax.dot_general(lhs[...], place, TRANSPOSED, preferred_element_type=F32)
        for xx in range(NX):
            for zz in range(2):
                part = out[xx * ROWS:(xx + 1) * ROWS, zz * 128:(zz + 1) * 128]
                sb[xx, pl.ds(2 * q + zz, 80, stride=8), :] = part[:80] + part[80:160]
                lb[xx, pl.ds(2 * q + zz, 8, stride=8), :] = part[160:168] + half
        return carry

    lax.fori_loop(0, 2, sort, 0)
    wait(gather_first())
    qa[pl.ds(pl.multiple_of(x * 24, 8), 24), :] = p0[pl.ds(0, 24), :]
    qb[pl.ds(pl.multiple_of(y * 24, 8), 24), :] = p0[pl.ds(24, 24), :]
    start(gather_second())
    lax.fori_loop(2, 4, sort, 0)
    wait(gather_second())
    ra[pl.ds(pl.multiple_of((core * NY + y) * 96, 8), 96), :] = qa[...]
    rb[pl.ds(pl.multiple_of((x * NC + core) * 96, 8), 96), :] = qb[...]
    start(gather_core())

    def cam_tile(xx, kk, c):
        return sb[xx, pl.ds((kk * 8 + c) * 8, 8), :]

    def spread(xx, zz, dense):
        gs = lax.broadcasted_iota(jnp.int32, (8, 128), 0).astype(F32)
        columns = []
        for k in range(TRACK):
            hit = gs == jnp.broadcast_to(lb[xx, pl.ds(k * 8 + zz, 1), :], (8, 128))
            tiles = []
            for part in range(2):
                for c in range(6):
                    row = vb[pl.ds(((part * TRACK + k) * 6 + c) * 8 + zz, 1), :]
                    tiles.append(jnp.where(hit, jnp.broadcast_to(row, (8, 128)), 0.0))
            columns.append(jnp.concatenate(tiles, axis=0).astype(BF16))
        left = jnp.concatenate(columns, axis=1)
        out = lax.dot_general(left, ohb[xx * 8 + zz], TRANSPOSED, preferred_element_type=F32)
        out = out[:48] + out[48:]
        for c in range(6):
            dense[pl.ds(xx * 384 + c * 8 + zz, 8, stride=48), :] = out[c * 8:c * 8 + 8]

    def hold(k, c, value):
        high = value.astype(BF16).astype(F32)
        vb[pl.ds((k * 6 + c) * 8, 8), :] = high
        vb[pl.ds(((TRACK + k) * 6 + c) * 8, 8), :] = value - high

    def grad_part(xx, carry):
        for k in range(TRACK):
            e0 = sb[xx, pl.ds((72 + 2 * k) * 8, 8), :]
            e1 = sb[xx, pl.ds((73 + 2 * k) * 8, 8), :]
            for c in range(6):
                hold(k, c, cam_tile(xx, 2 * k, c) * e0 + cam_tile(xx, 2 * k + 1, c) * e1)
        locals_of = lax.broadcasted_iota(jnp.int32, (128, 128), 0).astype(F32)
        for zz in range(NZ):
            for k in range(TRACK):
                label = lb[xx, pl.ds((4 + k) * 8 + zz, 1), :]
                ohb[xx * 8 + zz, :, pl.ds(k * 128, 128)] = (
                    locals_of == jnp.broadcast_to(label, (128, 128))
                ).astype(F32).astype(BF16)
            spread(xx, zz, gbuf)
        sum_core(24, gbuf, in1g, xx).start()
        return carry

    lax.fori_loop(0, NX, grad_part, 0)
    wait(gather_core())

    def schur_part(xx, carry):
        for zz in range(NZ):
            for c in range(3):
                tt[zz, pl.ds(c, 8, stride=8), :] = ra[pl.ds(xx * 24 + c * 8 + zz, 8, stride=96), :]
                tt[zz, pl.ds(3 + c, 8, stride=8), :] = (
                    rb[pl.ds(xx * 192 + c * 8 + zz, 8, stride=24), :]
                )
            high, low = split(tt[zz])
            onehot = ohb[xx * 8 + zz]
            got = jnp.dot(
                jnp.concatenate([high, low], axis=1),
                jnp.concatenate([onehot, onehot], axis=0),
                preferred_element_type=F32,
            )
            for k in range(TRACK):
                group = jnp.broadcast_to(lb[xx, pl.ds(k * 8 + zz, 1), :], (8, 128))
                mine = jnp.zeros((8, 128), F32)
                for g in range(8):
                    mine += jnp.where(
                        group == g, got[g * 8:g * 8 + 8, k * 128:(k + 1) * 128], 0.0
                    )
                db[pl.ds(k * 64 + zz, 8, stride=8), :] = mine
        image = []
        for k in range(TRACK):
            for i in range(2):
                image.append(
                    sum(
                        cam_tile(xx, 2 * k + i, c) * db[pl.ds((k * 8 + c) * 8, 8), :]
                        for c in range(6)
                    )
                )

        def point_tile(kk, j):
            at = kk * 8 + 6 + j if j < 2 else 64 + kk
            return sb[xx, pl.ds(at * 8, 8), :]

        through = [sum(point_tile(kk, j) * image[kk] for kk in range(8)) for j in range(3)]
        image = [image[kk] - sum(point_tile(kk, j) * through[j] for j in range(3)) for kk in range(8)]
        for k in range(TRACK):
            for c in range(6):
                hold(
                    k, c,
                    cam_tile(xx, 2 * k, c) * image[2 * k]
                    + cam_tile(xx, 2 * k + 1, c) * image[2 * k + 1],
                )
        for zz in range(NZ):
            spread(xx, zz, sbuf)
        sum_core(47, sbuf, in1s, xx).start()
        return carry

    def advance_first(base, dense, in1, r1a, r1b, in2a, in2b):
        wait([sum_core(base, dense, in1, xx) for xx in range(NX)])
        fold_core(dense, in1, r1a, r1b)
        start(sum_first(base, r1a, r1b, in2a, in2b))

    def advance_second(base, r1a, r1b, in2a, in2b, r2a, r2b, in3a, in3b):
        wait(sum_first(base, r1a, r1b, in2a, in2b))
        r2a[...] = fold(r1a, in2a, x, NX, 96)
        r2b[...] = fold(r1b, in2b, y, NY, 96)
        start(sum_second(base, r2a, r2b, in3a, in3b))

    def advance_z(base, r2a, r2b, in3a, in3b, r3, r4, in4):
        wait(sum_second(base, r2a, r2b, in3a, in3b))
        r3[pl.ds(0, 24), :] = fold(r2a, in3a, y, NY, 24)
        r3[pl.ds(24, 24), :] = fold(r2b, in3b, x, NX, 24)
        for zz in range(NZ):
            r4[pl.ds(zz * 8, 6), :] = r3[pl.ds(zz, 6, stride=8), :]
        start(sum_z(base, r4, in4))

    def finish(base, r4, in4):
        wait(sum_z(base, r4, in4))
        return fold(r4, in4, z, NZ, 8)[:6]

    lax.fori_loop(0, 1, schur_part, 0)
    advance_first(24, gbuf, in1g, r1ag, r1bg, in2ag, in2bg)
    lax.fori_loop(1, 3, schur_part, 0)
    advance_second(24, r1ag, r1bg, in2ag, in2bg, r2ag, r2bg, in3ag, in3bg)
    lax.fori_loop(3, NX, schur_part, 0)
    advance_z(24, r2ag, r2bg, in3ag, in3bg, r3g, r4g, in4g)
    advance_first(47, sbuf, in1s, r1as, r1bs, in2as, in2bs)
    og_ref[...] = finish(24, r4g, in4g)
    advance_second(47, r1as, r1bs, in2as, in2bs, r2as, r2bs, in3as, in3bs)
    advance_z(47, r2as, r2bs, in3as, in3bs, r3s, r4s, in4s)
    os_ref[...] = cdamp_ref[...] * dir_ref[...] + finish(47, r4s, in4s)


def shards(jac_cam, jac_pt, resid, point_damping, cluster, cam_local, direction, cam_damping):
    def buffer(*shape):
        return pltpu.VMEM(shape, F32)

    scratch = [
        buffer(POINTS // 128, 24, 128), buffer(8, POINTS), pltpu.VMEM((1, POINTS), jnp.int32),
        pltpu.VMEM((NX * ROWS, POINTS), BF16),
        buffer(NX, 640, 128), buffer(NX, 64, 128), buffer(256, 128), buffer(384, 128),
        pltpu.VMEM((32, 128, 512), BF16), buffer(8, 64, 128),
        buffer(64, 128), buffer(48, 128), buffer(96, 128), buffer(96, 128),
        buffer(768, 128), buffer(768, 128),
        buffer(1536, 128), buffer(1536, 128), buffer(768, 128), buffer(768, 128),
    ]
    scratch += [buffer(384, 128) for _ in range(8)]
    scratch += [buffer(96, 128) for _ in range(8)]
    scratch += [buffer(48, 128) for _ in range(2)]
    scratch += [buffer(64, 128) for _ in range(4)]
    scratch += [pltpu.SemaphoreType.DMA((70,)), pltpu.SemaphoreType.DMA((70,))]
    whole = pl.BlockSpec(memory_space=pltpu.VMEM)
    shape = jax.ShapeDtypeStruct((6, 128), F32)
    return pl.pallas_call(
        kernel,
        out_shape=(shape, shape),
        in_specs=[whole] * 8,
        out_specs=(whole, whole),
        scratch_shapes=scratch,
        compiler_params=pltpu.CompilerParams(
            collective_id=0, has_side_effects=True, vmem_limit_bytes=48 * 1024 * 1024
        ),
    )(
        jac_cam.reshape(8, 6, POINTS),
        jac_pt.reshape(8, 3, POINTS),
        resid,
        point_damping.reshape(1, POINTS),
        cluster.T,
        cam_local.T,
        direction,
        cam_damping.reshape(1, 128),
    )


def solution(mesh):
    in_specs = (
        P(None, None, None, ("pts", "cam")),
        P(None, None, None, ("pts", "cam")),
        P(None, None, ("pts", "cam")),
        P(("pts", "cam")),
        P(("pts", "cam"), None),
        P(("pts", "cam"), None),
        P(None, ("pts", "cam")),
        P(("pts", "cam")),
    )
    out_specs = (P(None, ("pts", "cam")), P(None, ("pts", "cam")))
    return jax.shard_map(shards, mesh=mesh, in_specs=in_specs, out_specs=out_specs, check_vma=False)
```

profile of v0, /device:TPU:2, one launch (start us, length us, event | category | flops | bytes accessed | tf_op | source)
XLA Modules:
  0.0 51.7 jit_solution(12193132392812824392)
XLA Ops:
  0.6 0.0 copy-start.6
  0.6 1.1 %copy.11 = f32[4,2,3,2048]{3,2,1,0:T(4,128)S(1)} copy(f32[4,2,3,2048]{3,1,2,0:T(2,128)} %param.9) | data formatting | bytes 393216 | tf_op args[1]
  1.8 0.0 copy-done.6
  1.8 0.0 copy-start
  1.8 0.0 copy-start.1
  1.8 0.0 copy-start.2
  1.8 0.0 copy-start.3
  1.8 0.0 copy-start.4
  1.8 0.2 copy.10
  2.1 0.0 copy-start.5
  2.1 0.5 %copy-done = f32[4,2,2048]{2,1,0:T(2,128)S(1)} copy-done((f32[4,2,2048]{2,1,0:T(2,128)S(1)}, f32[4,2,2048]{2,1,0:T(2,128)}, u32[]{:S(2)}) %copy-start) | copy-done | bytes 65560
  2.6 0.0 copy-done.1
  2.6 0.0 copy-done.2
  2.6 0.0 copy-done.3
  2.6 0.0 copy-done.4
  2.6 0.1 copy-done.5
  2.7 47.8 %shard_map.95 = (f32[6,128]{1,0:T(8,128)S(1)}, f32[6,128]{1,0:T(8,128)S(1)}) custom-call(f32[8,6,2048]{2,1,0:T(8,128)S(1)} %bitcast.6, f32[8,3,2048]{2,1,0:T(4,128)S(1)} %bitcast.7, f32[4,2,2048]{2,1,0:T(2,128)S(1)} %copy-done, f32[1,2048]{1,0:T(1,128)S(1)} %bitcast.9, s32[1,2048]{1,0:T(1,128)S(1)} %bitcast.10, s32[4,2048]{1,0:T(4,128)S(1)} %bitcast.8, ...), custom_call_target="tpu_custom_call" | custom-call | tf_op jit(solution)/shard_map/pallas_call | solution.py:425
  50.5 0.6 %copy.14 = f32[6,128]{1,0:T(8,128)} copy(f32[6,128]{1,0:T(8,128)S(1)} %get-tuple-element.4) | data formatting | bytes 6144
  51.1 0.6 %copy.15 = f32[6,128]{1,0:T(8,128)} copy(f32[6,128]{1,0:T(8,128)S(1)} %get-tuple-element.5) | data formatting | bytes 6144
Async XLA Ops:
  0.6 1.1 %copy-start.6 = (f32[4,2,6,2048]{3,1,2,0:T(2,128)S(1)}, f32[4,2,6,2048]{3,1,2,0:T(2,128)}, u32[]{:S(2)}) copy-start(f32[4,2,6,2048]{3,1,2,0:T(2,128)} %param.8) | copy-start | bytes 1179652
  1.8 0.8 %copy-start = (f32[4,2,2048]{2,1,0:T(2,128)S(1)}, f32[4,2,2048]{2,1,0:T(2,128)}, u32[]{:S(2)}) copy-start(f32[4,2,2048]{2,1,0:T(2,128)} %rs_ref.1) | copy-start | bytes 196612
  1.8 0.8 %copy-start.1 = (s32[2048,4]{0,1:T(4,128)S(1)}, s32[2048,4]{0,1:T(4,128)}, u32[]{:S(2)}) copy-start(s32[2048,4]{0,1:T(4,128)} %param.13) | copy-start | bytes 98308
  1.8 0.8 %copy-start.2 = (f32[2048]{0:T(1024)S(1)}, f32[2048]{0:T(1024)}, u32[]{:S(2)}) copy-start(f32[2048]{0:T(1024)} %param.11) | copy-start | bytes 24580
  1.8 0.8 %copy-start.3 = (s32[2048,1]{0,1:T(1,128)S(1)}, s32[2048,1]{0,1:T(1,128)}, u32[]{:S(2)}) copy-start(s32[2048,1]{0,1:T(1,128)} %param.12) | copy-start | bytes 24580
  1.8 0.8 %copy-start.4 = (f32[6,128]{1,0:T(8,128)S(1)}, f32[6,128]{1,0:T(8,128)}, u32[]{:S(2)}) copy-start(f32[6,128]{1,0:T(8,128)} %dir_ref.1) | copy-start | bytes 9220
  2.1 0.7 %copy-start.5 = (f32[128]{0:T(128)S(1)}, f32[128]{0:T(128)}, u32[]{:S(2)}) copy-start(f32[128]{0:T(128)} %param.15) | copy-start | bytes 1540
where the time goes:
time: 51.9 us; the launch traced here: 51.7 us
  Pallas kernels  47.8 us (92%)
  local copies, waits for them, and re-layouts  3.23 us (6%)
  between operations  0.72 us (1%)
    pallas_call x1, Pallas kernels, shards(): pl.pallas_call(kernel, out_shape=(shape, shape), in_specs=[whole] * 8, ou...  47.8 us
    unnamed x18, local copies, waits for them, and re-layouts  3.23 us

commit v1 on v0

v1 whole, which is shorter than its diff:
```python
import jax
import jax.numpy as jnp
from jax import lax
from jax.experimental import pallas as pl
from jax.experimental.pallas import tpu as pltpu
from jax.sharding import PartitionSpec as P

MESH = pl.DeviceIdType.MESH
F32 = jnp.float32
BF16 = jnp.bfloat16
NX, NY, NZ, NC = 4, 4, 8, 2
POINTS = 2048
CHUNK = 256
ROWS = 176
TRACK = 4
TRANSPOSED = (((1,), (1,)), ((), ()))


def split(value):
    high = value.astype(BF16)
    low = (value - high.astype(F32)).astype(BF16)
    return high, low


def kernel(
    jc_ref, jp_ref, rs_ref, damp_ref, clu_ref, loc_ref, dir_ref, cdamp_ref,
    os_ref,
    at, bt, rt, damp, clu, loc, own, cdamp,
    srow, lhs, sb, lb, db, vb, ohb, tt,
    zb, p0, dirs,
    gbuf, sbuf, in1g, in1s, r1g, r1s, in2g, in2s, r3, r4, in4,
    send, recv, fetch,
):
    me = lax.axis_index("pts")
    y = lax.axis_index("cam")
    core = lax.rem(me, NC)
    z = lax.rem(lax.div(me, NC), NZ)
    x = lax.div(me, NC * NZ)

    def device(xx, yy, zz, cc):
        return {"pts": (xx * NZ + zz) * NC + cc, "cam": yy}

    def step(at, d, size):
        return lax.rem(at + d, size)

    def rows(ref, start, count):
        return ref.at[pl.ds(pl.multiple_of(start, 8), count), :]

    def copy(src, dst, sem, dev):
        return pltpu.make_async_remote_copy(
            src_ref=src, dst_ref=dst, send_sem=send.at[sem], recv_sem=recv.at[sem],
            device_id=dev, device_id_type=MESH,
        )

    barrier = pltpu.get_barrier_semaphore()
    plane = [(r, d) for r in range(NX) for d in range(NY) if r + d > 0]
    peers = [device(x, y, step(z, d, NZ), core) for d in range(1, NZ)]
    peers += [device(step(x, r, NX), step(y, d, NY), z, core) for r, d in plane]
    peers += [device(x, y, z, 1 - core)]
    for dev in peers:
        pl.semaphore_signal(barrier, inc=1, device_id=dev, device_id_type=MESH)

    fetches = [(dir_ref, own), (clu_ref, clu), (loc_ref, loc), (damp_ref, damp), (cdamp_ref, cdamp)]
    fetches += [(rs_ref.at[k], rt.at[pl.ds(2 * k, 2), :]) for k in range(TRACK)]
    fetches += [
        (jp_ref.at[k, j], bt.at[pl.ds(8 * j + 2 * k, 2), :]) for k in range(TRACK) for j in range(3)
    ]
    fetches += [
        (jc_ref.at[k, c], at.at[pl.ds((k * 6 + c) * 2, 2), :]) for k in range(TRACK) for c in range(6)
    ]
    fetches = [
        pltpu.make_async_copy(src, dst, fetch.at[i]) for i, (src, dst) in enumerate(fetches)
    ]
    for item in fetches:
        item.start()
    tt[...] = jnp.zeros_like(tt)
    r4[...] = jnp.zeros_like(r4)

    def gather_z():
        return [
            copy(own, rows(zb, z * 8, 6), d - 1, device(x, y, step(z, d, NZ), core))
            for d in range(1, NZ)
        ]

    def gather_plane(r, d):
        there = device(step(x, r, NX), step(y, d, NY), z, core)
        return copy(p0, rows(dirs, ((x * NC + core) * NY + y) * 48, 48), 8 + r * NY + d, there)

    def gather_core(i, xx):
        part = rows(dirs, (xx * NC + core) * 192, 192)
        return copy(part, part, 24 + i, device(x, y, z, 1 - core))

    def sum_core(base, dense, in1, i, xx):
        return copy(
            rows(dense, (xx * NC + 1 - core) * 192, 192), rows(in1, xx * 192, 192),
            base + i, device(x, y, z, 1 - core),
        )

    def sum_plane(base, r1, in2, r, d):
        xx, yy = step(x, r, NX), step(y, d, NY)
        return copy(
            rows(r1, (xx * NY + yy) * 48, 48), rows(in2, (x * NY + y) * 48, 48),
            base + r * NY + d, device(xx, yy, z, core),
        )

    def sum_z():
        return [
            copy(rows(r4, step(z, d, NZ) * 16, 16), rows(in4, z * 16, 16), 68 + d,
                 device(x, y, step(z, d, NZ), core))
            for d in range(1, NZ)
        ]

    def turn(i):
        return i + i // 2 - 2 * (i // 3)

    fetches[0].wait()
    pl.semaphore_wait(barrier, len(peers))
    for item in gather_z():
        item.start()
    for item in fetches[1:]:
        item.wait()

    lane = lax.broadcasted_iota(jnp.int32, (CHUNK, CHUNK + 128), 1)
    before = (
        (lax.broadcasted_iota(jnp.int32, (CHUNK, CHUNK + 128), 0) < lane) | (lane >= CHUNK)
    ).astype(F32).astype(BF16)

    def eliminate(b, seen):
        here = pl.ds(pl.multiple_of(b * CHUNK, CHUNK), CHUNK)
        cluster = clu[:, here]
        member = (
            lax.broadcasted_iota(jnp.int32, (64, CHUNK), 0) == jnp.broadcast_to(cluster, (64, CHUNK))
        ).astype(F32)
        counts = jnp.dot(member.astype(BF16), before, preferred_element_type=F32)
        ahead = counts[:, :CHUNK] + jnp.concatenate([seen, seen], axis=1)
        position = jnp.sum(member * ahead, axis=0, keepdims=True)
        slot = jnp.bitwise_and(cluster, 15) * 64 + position.astype(jnp.int32)
        srow[:, here] = slot
        quarter = lax.shift_right_logical(cluster, 4)

        b0, b1, b2 = (bt[pl.ds(8 * j, 8), here] for j in range(3))
        res = rt[:, here]

        def total(value):
            return jnp.sum(value, axis=0, keepdims=True)

        extra = damp[:, here]
        n00, n10, n20 = total(b0 * b0) + extra, total(b1 * b0), total(b2 * b0)
        n11, n21, n22 = total(b1 * b1) + extra, total(b2 * b1), total(b2 * b2) + extra
        q0, q1, q2 = total(b0 * res), total(b1 * res), total(b2 * res)
        ia = 1.0 / jnp.sqrt(n00)
        ba, ca = n10 * ia, n20 * ia
        ib = 1.0 / jnp.sqrt(n11 - ba * ba)
        cb = (n21 - ca * ba) * ib
        ic = 1.0 / jnp.sqrt(n22 - ca * ca - cb * cb)
        c0 = b0 * ia
        c1 = (b1 - ba * c0) * ib
        c2 = (b2 - ca * c0 - cb * c1) * ic
        s0 = q0 * ia
        s1 = (q1 - ba * s0) * ib
        s2 = (q2 - ca * s0 - cb * s1) * ic
        rest = res - (c0 * s0 + c1 * s1 + c2 * s2)

        masks = [
            jnp.broadcast_to((quarter == f).astype(F32), (16, CHUNK)).astype(BF16)
            for f in range(NX)
        ]

        def put(base, value):
            for f in range(NX):
                lhs[pl.ds(f * ROWS + base, 16), here] = value * masks[f]

        for base in range(0, 48, 16):
            high, low = split(at[pl.ds(base, 16), here])
            put(base, high)
            put(80 + base, low)
        for base, pair in ((48, (c0, c1)), (64, (c2, rest))):
            high, low = split(jnp.concatenate(pair, axis=0))
            put(base, high)
            put(80 + base, low)
        label = loc[:, here]
        parts = [
            lax.shift_right_logical(label, 7).astype(F32),
            jnp.bitwise_and(label, 127).astype(F32),
            jnp.zeros((8, CHUNK), F32),
        ]
        put(160, jnp.concatenate(parts, axis=0).astype(BF16))
        return seen + counts[:, CHUNK:]

    lax.fori_loop(0, POINTS // CHUNK, eliminate, jnp.zeros((64, 128), F32))

    half = jnp.where(lax.broadcasted_iota(jnp.int32, (8, 128), 1) >= 64, 4.0, 0.0)
    half = jnp.where(lax.broadcasted_iota(jnp.int32, (8, 128), 0) < 4, half, 0.0)

    def sort(q, carry):
        slots = lax.broadcasted_iota(jnp.int32, (256, POINTS), 0) + q * 256
        place = (slots == jnp.broadcast_to(srow[...], (256, POINTS))).astype(F32).astype(BF16)
        out = lax.dot_general(lhs[...], place, TRANSPOSED, preferred_element_type=F32)
        for xx in range(NX):
            for zz in range(2):
                part = out[xx * ROWS:(xx + 1) * ROWS, zz * 128:(zz + 1) * 128]
                sb[xx, pl.ds(2 * q + zz, 80, stride=8), :] = part[:80] + part[80:160]
                lb[xx, pl.ds(2 * q + zz, 8, stride=8), :] = part[160:168] + half
        return carry

    lax.fori_loop(0, 2, sort, 0)
    for item in gather_z():
        item.wait()
    zb[pl.ds(pl.multiple_of(z * 8, 8), 6), :] = own[...]
    for zz in range(NZ):
        p0[pl.ds(zz, 6, stride=8), :] = zb[pl.ds(zz * 8, 6), :]
    for r, d in plane:
        gather_plane(r, d).start()
    dirs[pl.ds(pl.multiple_of(((x * NC + core) * NY + y) * 48, 8), 48), :] = p0[...]
    lax.fori_loop(2, 4, sort, 0)

    def cam_tile(xx, kk, c):
        return sb[xx, pl.ds(((kk // 2 * 6 + c) * 2 + kk % 2) * 8, 8), :]

    def spread(xx, zz, dense):
        gs = lax.broadcasted_iota(jnp.int32, (8, 128), 0).astype(F32)
        columns = []
        for k in range(TRACK):
            hit = gs == jnp.broadcast_to(lb[xx, pl.ds(k * 8 + zz, 1), :], (8, 128))
            tiles = []
            for part in range(2):
                for c in range(6):
                    row = vb[pl.ds(((part * TRACK + k) * 6 + c) * 8 + zz, 1), :]
                    tiles.append(jnp.where(hit, jnp.broadcast_to(row, (8, 128)), 0.0))
            columns.append(jnp.concatenate(tiles, axis=0).astype(BF16))
        left = jnp.concatenate(columns, axis=1)
        out = lax.dot_general(left, ohb[xx * 8 + zz], TRANSPOSED, preferred_element_type=F32)
        out = out[:48] + out[48:]
        for c in range(6):
            dense[pl.ds(xx * 384 + c * 8 + zz, 8, stride=48), :] = out[c * 8:c * 8 + 8]

    def hold(k, c, value):
        high = value.astype(BF16).astype(F32)
        vb[pl.ds((k * 6 + c) * 8, 8), :] = high
        vb[pl.ds(((TRACK + k) * 6 + c) * 8, 8), :] = value - high

    def grad_part(i, carry):
        xx = step(x, turn(i), NX)
        for k in range(TRACK):
            e0 = sb[xx, pl.ds((72 + 2 * k) * 8, 8), :]
            e1 = sb[xx, pl.ds((73 + 2 * k) * 8, 8), :]
            for c in range(6):
                hold(k, c, cam_tile(xx, 2 * k, c) * e0 + cam_tile(xx, 2 * k + 1, c) * e1)
        locals_of = lax.broadcasted_iota(jnp.int32, (128, 128), 0).astype(F32)
        for zz in range(NZ):
            for k in range(TRACK):
                label = lb[xx, pl.ds((4 + k) * 8 + zz, 1), :]
                ohb[xx * 8 + zz, :, pl.ds(k * 128, 128)] = (
                    locals_of == jnp.broadcast_to(label, (128, 128))
                ).astype(F32).astype(BF16)
            spread(xx, zz, gbuf)
        sum_core(28, gbuf, in1g, i, xx).start()
        return carry

    def schur(xx):
        for zz in range(NZ):
            for c in range(6):
                tt[zz, pl.ds(c, 8, stride=8), :] = dirs[pl.ds(xx * 384 + c * 8 + zz, 8, stride=48), :]
            high, low = split(tt[zz])
            onehot = ohb[xx * 8 + zz]
            got = jnp.dot(
                jnp.concatenate([high, low], axis=1),
                jnp.concatenate([onehot, onehot], axis=0),
                preferred_element_type=F32,
            )
            for k in range(TRACK):
                group = jnp.broadcast_to(lb[xx, pl.ds(k * 8 + zz, 1), :], (8, 128))
                mine = jnp.zeros((8, 128), F32)
                for g in range(8):
                    mine += jnp.where(
                        group == g, got[g * 8:g * 8 + 8, k * 128:(k + 1) * 128], 0.0
                    )
                db[pl.ds(k * 64 + zz, 8, stride=8), :] = mine
        image = []
        for k in range(TRACK):
            for i in range(2):
                image.append(
                    sum(
                        cam_tile(xx, 2 * k + i, c) * db[pl.ds((k * 8 + c) * 8, 8), :]
                        for c in range(6)
                    )
                )

        def point_tile(kk, j):
            return sb[xx, pl.ds((48 + j * 8 + kk) * 8, 8), :]

        through = [sum(point_tile(kk, j) * image[kk] for kk in range(8)) for j in range(3)]
        image = [image[kk] - sum(point_tile(kk, j) * through[j] for j in range(3)) for kk in range(8)]
        for k in range(TRACK):
            for c in range(6):
                hold(
                    k, c,
                    cam_tile(xx, 2 * k, c) * image[2 * k]
                    + cam_tile(xx, 2 * k + 1, c) * image[2 * k + 1],
                )
        for zz in range(NZ):
            spread(xx, zz, sbuf)

    lax.fori_loop(0, NX, grad_part, 0)

    def pass_on(i):
        r = turn(i)
        xx = step(x, r, NX)
        for d in range(NY):
            sent = 8 + lax.rem(NX - r, NX) * NY + (NY - d) % NY
            yy = step(y, d, NY)
            part = rows(dirs, ((xx * NC + core) * NY + yy) * 48, 48)

            def arrive():
                copy(p0, part, sent, device(xx, yy, z, core)).wait_recv()

            if d == 0:
                pl.when(i > 0)(arrive)
            else:
                arrive()
        gather_core(i, xx).start()

    def send_blocks(base1, base2, dense, in1, r1, in2, i):
        r = turn(i)
        xx = step(x, r, NX)
        sum_core(base1, dense, in1, i, xx).wait()
        here = pl.ds(pl.multiple_of(xx * 192, 8), 192)
        r1[here, :] = dense[pl.ds(pl.multiple_of((xx * NC + core) * 192, 8), 192), :] + in1[here, :]
        for d in range(NY):
            item = sum_plane(base2, r1, in2, r, d)
            if d == 0:
                pl.when(i > 0)(item.start)
            else:
                item.start()

    def schur_part(i, carry):
        xx = step(x, turn(i), NX)

        @pl.when(i < NX - 1)
        def _():
            pass_on(i + 1)

        send_blocks(28, 36, gbuf, in1g, r1g, in2g, i)
        gather_core(i, xx).wait()
        schur(xx)
        sum_core(32, sbuf, in1s, i, xx).start()

        @pl.when(i > 0)
        def _():
            send_blocks(32, 52, sbuf, in1s, r1s, in2s, i - 1)

        return carry

    pass_on(0)
    lax.fori_loop(0, NX, schur_part, 0)
    send_blocks(32, 52, sbuf, in1s, r1s, in2s, NX - 1)

    def fold_plane(base, r1, in2):
        total = r1[pl.ds(pl.multiple_of((x * NY + y) * 48, 8), 48), :]
        for r, d in plane:
            sum_plane(base, r1, in2, r, d).wait()
            source = step(x, NX - r, NX) * NY + step(y, NY - d, NY)
            total += in2[pl.ds(pl.multiple_of(source * 48, 8), 48), :]
        return total

    for part, total in enumerate((fold_plane(36, r1g, in2g), fold_plane(52, r1s, in2s))):
        r3[...] = total
        for zz in range(NZ):
            r4[pl.ds(zz * 16 + 8 * part, 6), :] = r3[pl.ds(zz, 6, stride=8), :]
    for item in sum_z():
        item.start()
    total = r4[pl.ds(pl.multiple_of(z * 16, 8), 16), :]
    for d, item in enumerate(sum_z()):
        item.wait()
        total += in4[pl.ds(pl.multiple_of(step(z, NZ - 1 - d, NZ) * 16, 8), 16), :]
    for r, d in plane:
        gather_plane(r, d).wait_send()
    os_ref[...] = total


def shards(jac_cam, jac_pt, resid, point_damping, cluster, cam_local, direction, cam_damping):
    def buffer(*shape):
        return pltpu.VMEM(shape, F32)

    scratch = [
        buffer(48, POINTS), buffer(24, POINTS), buffer(8, POINTS), buffer(1, POINTS),
        pltpu.VMEM((1, POINTS), jnp.int32), pltpu.VMEM((TRACK, POINTS), jnp.int32),
        buffer(6, 128), buffer(1, 128),
        pltpu.VMEM((1, POINTS), jnp.int32), pltpu.VMEM((NX * ROWS, POINTS), BF16),
        buffer(NX, 640, 128), buffer(NX, 64, 128), buffer(256, 128), buffer(384, 128),
        pltpu.VMEM((32, 128, 512), BF16), buffer(8, 64, 128),
        buffer(64, 128), buffer(48, 128), buffer(1536, 128),
        buffer(1536, 128), buffer(1536, 128), buffer(768, 128), buffer(768, 128),
        buffer(768, 128), buffer(768, 128), buffer(768, 128), buffer(768, 128),
        buffer(48, 128), buffer(128, 128), buffer(128, 128),
        pltpu.SemaphoreType.DMA((76,)), pltpu.SemaphoreType.DMA((76,)),
        pltpu.SemaphoreType.DMA((45,)),
    ]
    whole = pl.BlockSpec(memory_space=pltpu.VMEM)
    shape = jax.ShapeDtypeStruct((6, 128), F32)
    both = pl.pallas_call(
        kernel,
        out_shape=jax.ShapeDtypeStruct((16, 128), F32),
        in_specs=[pl.BlockSpec(memory_space=pltpu.HBM)] * 8,
        out_specs=whole,
        scratch_shapes=scratch,
        compiler_params=pltpu.CompilerParams(
            collective_id=0, has_side_effects=True, vmem_limit_bytes=62 * 1024 * 1024
        ),
    )(
        jnp.transpose(jac_cam, (0, 2, 1, 3)),
        jnp.transpose(jac_pt, (0, 2, 1, 3)),
        resid,
        point_damping.reshape(1, POINTS),
        cluster.T,
        cam_local.T,
        direction,
        cam_damping.reshape(1, 128),
    )
    return both[:6], cam_damping[None, :] * direction + both[8:14]


def solution(mesh):
    in_specs = (
        P(None, None, None, ("pts", "cam")),
        P(None, None, None, ("pts", "cam")),
        P(None, None, ("pts", "cam")),
        P(("pts", "cam")),
        P(("pts", "cam"), None),
        P(("pts", "cam"), None),
        P(None, ("pts", "cam")),
        P(("pts", "cam")),
    )
    out_specs = (P(None, ("pts", "cam")), P(None, ("pts", "cam")))
    return jax.shard_map(shards, mesh=mesh, in_specs=in_specs, out_specs=out_specs, check_vma=False)
```

time: 51.9 us -> 44.4 us (0.86)
  Pallas kernels: 47.8 us -> 42.3 us
  local copies, waits for them, and re-layouts: 3.23 us -> 0.01 us
  other arithmetic: 0 us -> 1.29 us
    pallas_call x1, Pallas kernels: 47.8 us -> 42.3 us  [shards(): pl.pallas_call(kernel, out_shape=jax.ShapeDtypeStruct((16, 128), F32), in...]
    unnamed x18 -> x4, local copies, waits for them, and re-layouts: 3.23 us -> 0.01 us
    add x0 -> x1, other arithmetic: none -> 1.29 us  [shards(): return (both[:6], cam_damping[None, :] * direction + both[8:14])]
where the time goes in v1:
time: 44.4 us; the launch traced here: 44.3 us
  Pallas kernels  42.3 us (95%)
  other arithmetic  1.29 us (3%)
  between operations  0.67 us (2%)
    pallas_call x1, Pallas kernels, shards(): pl.pallas_call(kernel, out_shape=jax.ShapeDtypeStruct((16, 128), F32), in...  42.3 us
    add x1, other arithmetic, shards(): return (both[:6], cam_damping[None, :] * direction + both[8:14])  1.29 us

profile of v1, /device:TPU:2, one launch (start us, length us, event | category | flops | bytes accessed | tf_op | source)
XLA Modules:
  0.0 44.3 jit_solution(2336073741964197270)
XLA Ops:
  0.6 0.0 copy-start
  0.6 0.0 copy-start.1
  0.7 42.3 %shard_map.95 = f32[16,128]{1,0:T(8,128)} custom-call(f32[4,6,2,2048]{3,2,1,0:T(2,128)} %bitcast.6, f32[4,3,2,2048]{3,2,1,0:T(2,128)} %bitcast.7, f32[4,2,2048]{2,1,0:T(2,128)} %rs_ref.1, f32[1,2048]{1,0:T(1,128)} %bitcast.9, s32[1,2048]{1,0:T(1,128)} %bitcast.10, s32[4,2048]{1,0:T(4,128)} %bitcast.8, f32[6,128]{1,0:T(8,128)} %dir_ref.1, f32[1,128]{1,0:T(1,128)} %bitcast.11), custom_call_target="tpu_custom_call" | custom-call | tf_op jit(solution)/shard_map/pallas_call | solution.py:401
  43.0 0.0 copy-done
  43.0 0.0 copy-done.1
  43.0 1.3 %slice_add_fusion = (f32[6,128]{1,0:T(8,128)}, f32[6,128]{1,0:T(8,128)}) fusion(f32[16,128]{1,0:T(8,128)} %shard_map.95, f32[6,128]{1,0:T(8,128)S(1)} %copy-done, f32[128]{0:T(128)S(1)} %copy-done.1), kind=kLoop, calls=%fused_computation | loop fusion | flops 1536 | bytes 15872 | tf_op jit(solution)/shard_map/add | solution.py:420
Async XLA Ops:
  0.6 42.3 %copy-start = (f32[6,128]{1,0:T(8,128)S(1)}, f32[6,128]{1,0:T(8,128)}, u32[]{:S(2)}) copy-start(f32[6,128]{1,0:T(8,128)} %dir_ref.1) | copy-start | bytes 9220
  0.6 42.3 %copy-start.1 = (f32[128]{0:T(128)S(1)}, f32[128]{0:T(128)}, u32[]{:S(2)}) copy-start(f32[128]{0:T(128)} %param.15) | copy-start | bytes 1540

commit v2 on v1

--- a/solution.py
+++ b/solution.py
@@ -78,8 +78,8 @@
 
     def gather_z():
         return [
-            copy(own, rows(zb, z * 8, 6), d - 1, device(x, y, step(z, d, NZ), core))
-            for d in range(1, NZ)
+            copy(dir_ref, rows(zb, z * 8, 6), d - 1, device(x, y, step(z, d, NZ), core))
+            for d in (4, 3, 5, 2, 6, 1, 7)
         ]
 
     def gather_plane(r, d):
@@ -107,17 +107,16 @@
         return [
             copy(rows(r4, step(z, d, NZ) * 16, 16), rows(in4, z * 16, 16), 68 + d,
                  device(x, y, step(z, d, NZ), core))
-            for d in range(1, NZ)
+            for d in (4, 3, 5, 2, 6, 1, 7)
         ]
 
     def turn(i):
         return i + i // 2 - 2 * (i // 3)
 
-    fetches[0].wait()
     pl.semaphore_wait(barrier, len(peers))
     for item in gather_z():
         item.start()
-    for item in fetches[1:]:
+    for item in fetches:
         item.wait()
 
     lane = lax.broadcasted_iota(jnp.int32, (CHUNK, CHUNK + 128), 1)
@@ -209,8 +208,10 @@
     zb[pl.ds(pl.multiple_of(z * 8, 8), 6), :] = own[...]
     for zz in range(NZ):
         p0[pl.ds(zz, 6, stride=8), :] = zb[pl.ds(zz * 8, 6), :]
-    for r, d in plane:
-        gather_plane(r, d).start()
+    for r in (0, 1, 3, 2):
+        for d in (2, 1, 3, 0):
+            if r + d > 0:
+                gather_plane(r, d).start()
     dirs[pl.ds(pl.multiple_of(((x * NC + core) * NY + y) * 48, 8), 48), :] = p0[...]
     lax.fori_loop(2, 4, sort, 0)
 
@@ -303,21 +304,20 @@
 
     lax.fori_loop(0, NX, grad_part, 0)
 
+    def own_group():
+        for d in range(1, NY):
+            part = rows(dirs, ((x * NC + core) * NY + step(y, d, NY)) * 48, 48)
+            copy(p0, part, 8 + NY - d, device(x, step(y, d, NY), z, core)).wait_recv()
+        gather_core(0, x).start()
+
     def pass_on(i):
         r = turn(i)
         xx = step(x, r, NX)
         for d in range(NY):
-            sent = 8 + lax.rem(NX - r, NX) * NY + (NY - d) % NY
+            sent = 8 + (NX - r) * NY + (NY - d) % NY
             yy = step(y, d, NY)
             part = rows(dirs, ((xx * NC + core) * NY + yy) * 48, 48)
-
-            def arrive():
-                copy(p0, part, sent, device(xx, yy, z, core)).wait_recv()
-
-            if d == 0:
-                pl.when(i > 0)(arrive)
-            else:
-                arrive()
+            copy(p0, part, sent, device(xx, yy, z, core)).wait_recv()
         gather_core(i, xx).start()
 
     def send_blocks(base1, base2, dense, in1, r1, in2, i):
@@ -326,7 +326,7 @@
         sum_core(base1, dense, in1, i, xx).wait()
         here = pl.ds(pl.multiple_of(xx * 192, 8), 192)
         r1[here, :] = dense[pl.ds(pl.multiple_of((xx * NC + core) * 192, 8), 192), :] + in1[here, :]
-        for d in range(NY):
+        for d in (2, 1, 3, 0):
             item = sum_plane(base2, r1, in2, r, d)
             if d == 0:
                 pl.when(i > 0)(item.start)
@@ -336,43 +336,66 @@
     def schur_part(i, carry):
         xx = step(x, turn(i), NX)
 
-        @pl.when(i < NX - 1)
+        @pl.when(i < 2)
         def _():
-            pass_on(i + 1)
-
+            pass_on(i + 2)
+
+        gather_core(i, xx).wait()
+
+        schur(xx)
+
+        sum_core(32, sbuf, in1s, i, xx).start()
+
+        @pl.when(i >= 2)
+        def _():
+            send_blocks(32, 52, sbuf, in1s, r1s, in2s, i - 2)
+
+        return carry
+
+    def send_grad(i, carry):
         send_blocks(28, 36, gbuf, in1g, r1g, in2g, i)
-        gather_core(i, xx).wait()
-        schur(xx)
-        sum_core(32, sbuf, in1s, i, xx).start()
-
-        @pl.when(i > 0)
-        def _():
-            send_blocks(32, 52, sbuf, in1s, r1s, in2s, i - 1)
-
         return carry
 
-    pass_on(0)
+    own_group()
+    pass_on(1)
+    lax.fori_loop(0, NX, send_grad, 0)
     lax.fori_loop(0, NX, schur_part, 0)
-    send_blocks(32, 52, sbuf, in1s, r1s, in2s, NX - 1)
-
-    def fold_plane(base, r1, in2):
-        total = r1[pl.ds(pl.multiple_of((x * NY + y) * 48, 8), 48), :]
+    send_blocks(32, 52, sbuf, in1s, r1s, in2s, 2)
+    send_blocks(32, 52, sbuf, in1s, r1s, in2s, 3)
+
+    def block(at):
+        return pl.ds(pl.multiple_of(at * 48, 8), 48)
+
+    def from_source(r, d):
+        return block(step(x, NX - r, NX) * NY + step(y, NY - d, NY))
+
+    def fold_grad():
+        total = r1g[block(x * NY + y), :]
         for r, d in plane:
-            sum_plane(base, r1, in2, r, d).wait()
-            source = step(x, NX - r, NX) * NY + step(y, NY - d, NY)
-            total += in2[pl.ds(pl.multiple_of(source * 48, 8), 48), :]
+            sum_plane(36, r1g, in2g, r, d).wait()
+            total += in2g[from_source(r, d), :]
         return total
 
-    for part, total in enumerate((fold_plane(36, r1g, in2g), fold_plane(52, r1s, in2s))):
+    def fold_prod():
+        total = r1s[block(x * NY + y), :]
+        for r in (0, 1, 3, 2):
+            for d in range(NY):
+                if r + d > 0:
+                    sum_plane(52, r1s, in2s, r, d).wait()
+                    total += in2s[from_source(r, d), :]
+        return total
+
+    for part, total in enumerate((fold_grad(), fold_prod())):
         r3[...] = total
         for zz in range(NZ):
             r4[pl.ds(zz * 16 + 8 * part, 6), :] = r3[pl.ds(zz, 6, stride=8), :]
     for item in sum_z():
         item.start()
     total = r4[pl.ds(pl.multiple_of(z * 16, 8), 16), :]
-    for d, item in enumerate(sum_z()):
+    for item in sum_z():
         item.wait()
-        total += in4[pl.ds(pl.multiple_of(step(z, NZ - 1 - d, NZ) * 16, 8), 16), :]
+    for d in range(1, NZ):
+        total += in4[pl.ds(pl.multiple_of(step(z, d, NZ) * 16, 8), 16), :]
     for r, d in plane:
         gather_plane(r, d).wait_send()
     os_ref[...] = total

time: 44.4 us -> 41.5 us (0.935)
  the two profiles are of different devices: /device:TPU:2 before, /device:TPU:1 now
where the time goes in v2:
time: 41.5 us; the launch traced here: 41.3 us
  Pallas kernels  39.4 us (95%)
  other arithmetic  1.29 us (3%)
  between operations  0.67 us (2%)
    pallas_call x1, Pallas kernels, shards(): pl.pallas_call(kernel, out_shape=jax.ShapeDtypeStruct((16, 128), F32), in...  39.4 us
    add x1, other arithmetic, shards(): return (both[:6], cam_damping[None, :] * direction + both[8:14])  1.29 us

profile of v2, /device:TPU:1, one launch (start us, length us, event | category | flops | bytes accessed | tf_op | source)
XLA Modules:
  0.0 41.3 jit_solution(14440069307273171673)
XLA Ops:
  0.6 0.0 copy-start
  0.6 0.0 copy-start.1
  0.7 39.4 %shard_map.95 = f32[16,128]{1,0:T(8,128)} custom-call(f32[4,6,2,2048]{3,2,1,0:T(2,128)} %bitcast.6, f32[4,3,2,2048]{3,2,1,0:T(2,128)} %bitcast.7, f32[4,2,2048]{2,1,0:T(2,128)} %rs_ref.1, f32[1,2048]{1,0:T(1,128)} %bitcast.9, s32[1,2048]{1,0:T(1,128)} %bitcast.10, s32[4,2048]{1,0:T(4,128)} %bitcast.8, f32[6,128]{1,0:T(8,128)} %dir_ref.1, f32[1,128]{1,0:T(1,128)} %bitcast.11), custom_call_target="tpu_custom_call" | custom-call | tf_op jit(solution)/shard_map/pallas_call | solution.py:424
  40.0 0.0 copy-done
  40.1 0.0 copy-done.1
  40.1 1.3 %slice_add_fusion = (f32[6,128]{1,0:T(8,128)}, f32[6,128]{1,0:T(8,128)}) fusion(f32[16,128]{1,0:T(8,128)} %shard_map.95, f32[6,128]{1,0:T(8,128)S(1)} %copy-done, f32[128]{0:T(128)S(1)} %copy-done.1), kind=kLoop, calls=%fused_computation | loop fusion | flops 1536 | bytes 15872 | tf_op jit(solution)/shard_map/add | solution.py:443
Async XLA Ops:
  0.6 39.4 %copy-start = (f32[6,128]{1,0:T(8,128)S(1)}, f32[6,128]{1,0:T(8,128)}, u32[]{:S(2)}) copy-start(f32[6,128]{1,0:T(8,128)} %dir_ref.1) | copy-start | bytes 9220
  0.6 39.4 %copy-start.1 = (f32[128]{0:T(128)S(1)}, f32[128]{0:T(128)}, u32[]{:S(2)}) copy-start(f32[128]{0:T(128)} %param.15) | copy-start | bytes 1540

commit v3 on v2

--- a/solution.py
+++ b/solution.py
@@ -54,8 +54,12 @@
 
     barrier = pltpu.get_barrier_semaphore()
     plane = [(r, d) for r in range(NX) for d in range(NY) if r + d > 0]
-    peers = [device(x, y, step(z, d, NZ), core) for d in range(1, NZ)]
-    peers += [device(step(x, r, NX), step(y, d, NY), z, core) for r, d in plane]
+    peers = [device(x, y, step(z, d, NZ), core) for d in (4, 3, 5)]
+    peers += [
+        device(step(x, r, NX), step(y, d, NY), z, core)
+        for r in (2, 1, 3, 0) for d in (2, 1, 3, 0) if r + d > 0
+    ]
+    peers += [device(x, y, step(z, d, NZ), core) for d in (2, 6, 1, 7)]
     peers += [device(x, y, z, 1 - core)]
     for dev in peers:
         pl.semaphore_signal(barrier, inc=1, device_id=dev, device_id_type=MESH)
@@ -111,7 +115,7 @@
         ]
 
     def turn(i):
-        return i + i // 2 - 2 * (i // 3)
+        return (i + 1) % NX
 
     pl.semaphore_wait(barrier, len(peers))
     for item in gather_z():
@@ -304,20 +308,18 @@
 
     lax.fori_loop(0, NX, grad_part, 0)
 
-    def own_group():
-        for d in range(1, NY):
-            part = rows(dirs, ((x * NC + core) * NY + step(y, d, NY)) * 48, 48)
-            copy(p0, part, 8 + NY - d, device(x, step(y, d, NY), z, core)).wait_recv()
-        gather_core(0, x).start()
-
     def pass_on(i):
         r = turn(i)
         xx = step(x, r, NX)
         for d in range(NY):
-            sent = 8 + (NX - r) * NY + (NY - d) % NY
+            sent = 8 + (NX - r) % NX * NY + (NY - d) % NY
             yy = step(y, d, NY)
             part = rows(dirs, ((xx * NC + core) * NY + yy) * 48, 48)
-            copy(p0, part, sent, device(xx, yy, z, core)).wait_recv()
+            arrived = copy(p0, part, sent, device(xx, yy, z, core)).wait_recv
+            if d == 0:
+                pl.when(r > 0)(arrived)
+            else:
+                arrived()
         gather_core(i, xx).start()
 
     def send_blocks(base1, base2, dense, in1, r1, in2, i):
@@ -329,7 +331,7 @@
         for d in (2, 1, 3, 0):
             item = sum_plane(base2, r1, in2, r, d)
             if d == 0:
-                pl.when(i > 0)(item.start)
+                pl.when(r > 0)(item.start)
             else:
                 item.start()
 
@@ -356,7 +358,7 @@
         send_blocks(28, 36, gbuf, in1g, r1g, in2g, i)
         return carry
 
-    own_group()
+    pass_on(0)
     pass_on(1)
     lax.fori_loop(0, NX, send_grad, 0)
     lax.fori_loop(0, NX, schur_part, 0)

time: 41.5 us -> 40.7 us (0.981)
  the two profiles are of different devices: /device:TPU:1 before, /device:TPU:2 now
where the time goes in v3:
time: 40.7 us; the launch traced here: 40.5 us
  Pallas kernels  38.6 us (95%)
  other arithmetic  1.29 us (3%)
  between operations  0.67 us (2%)
    pallas_call x1, Pallas kernels, shards(): pl.pallas_call(kernel, out_shape=jax.ShapeDtypeStruct((16, 128), F32), in...  38.6 us
    add x1, other arithmetic, shards(): return (both[:6], cam_damping[None, :] * direction + both[8:14])  1.29 us

profile of v3, /device:TPU:2, one launch (start us, length us, event | category | flops | bytes accessed | tf_op | source)
XLA Modules:
  0.0 40.5 jit_solution(9029113048285024577)
XLA Ops:
  0.6 0.0 copy-start
  0.6 0.0 copy-start.1
  0.7 38.6 %shard_map.95 = f32[16,128]{1,0:T(8,128)} custom-call(f32[4,6,2,2048]{3,2,1,0:T(2,128)} %bitcast.6, f32[4,3,2,2048]{3,2,1,0:T(2,128)} %bitcast.7, f32[4,2,2048]{2,1,0:T(2,128)} %rs_ref.1, f32[1,2048]{1,0:T(1,128)} %bitcast.9, s32[1,2048]{1,0:T(1,128)} %bitcast.10, s32[4,2048]{1,0:T(4,128)} %bitcast.8, f32[6,128]{1,0:T(8,128)} %dir_ref.1, f32[1,128]{1,0:T(1,128)} %bitcast.11), custom_call_target="tpu_custom_call" | custom-call | tf_op jit(solution)/shard_map/pallas_call | solution.py:426
  39.2 0.0 copy-done
  39.2 0.0 copy-done.1
  39.3 1.3 %slice_add_fusion = (f32[6,128]{1,0:T(8,128)}, f32[6,128]{1,0:T(8,128)}) fusion(f32[16,128]{1,0:T(8,128)} %shard_map.95, f32[6,128]{1,0:T(8,128)S(1)} %copy-done, f32[128]{0:T(128)S(1)} %copy-done.1), kind=kLoop, calls=%fused_computation | loop fusion | flops 1536 | bytes 15872 | tf_op jit(solution)/shard_map/add | solution.py:445
Async XLA Ops:
  0.6 38.6 %copy-start = (f32[6,128]{1,0:T(8,128)S(1)}, f32[6,128]{1,0:T(8,128)}, u32[]{:S(2)}) copy-start(f32[6,128]{1,0:T(8,128)} %dir_ref.1) | copy-start | bytes 9220
  0.6 38.6 %copy-start.1 = (f32[128]{0:T(128)S(1)}, f32[128]{0:T(128)}, u32[]{:S(2)}) copy-start(f32[128]{0:T(128)} %param.15) | copy-start | bytes 1540

commit v4 on v3

--- a/solution.py
+++ b/solution.py
@@ -115,7 +115,7 @@
         ]
 
     def turn(i):
-        return (i + 1) % NX
+        return (i + 2) % NX
 
     pl.semaphore_wait(barrier, len(peers))
     for item in gather_z():
@@ -212,7 +212,7 @@
     zb[pl.ds(pl.multiple_of(z * 8, 8), 6), :] = own[...]
     for zz in range(NZ):
         p0[pl.ds(zz, 6, stride=8), :] = zb[pl.ds(zz * 8, 6), :]
-    for r in (0, 1, 3, 2):
+    for r in (2, 1, 3, 0):
         for d in (2, 1, 3, 0):
             if r + d > 0:
                 gather_plane(r, d).start()

time: 40.7 us -> 40.6 us (level)
  no operation moved by 1% of the time
where the time goes in v4:
time: 40.6 us; the launch traced here: 40.2 us
  Pallas kernels  38.3 us (94%)
  other arithmetic  1.29 us (3%)
  between operations  0.67 us (2%)
    pallas_call x1, Pallas kernels, shards(): pl.pallas_call(kernel, out_shape=jax.ShapeDtypeStruct((16, 128), F32), in...  38.3 us
    add x1, other arithmetic, shards(): return (both[:6], cam_damping[None, :] * direction + both[8:14])  1.29 us

profile of v4, /device:TPU:2, one launch (start us, length us, event | category | flops | bytes accessed | tf_op | source)
XLA Modules:
  0.0 40.2 jit_solution(13628979932752525613)
XLA Ops:
  0.6 0.0 copy-start
  0.6 0.0 copy-start.1
  0.7 38.3 %shard_map.95 = f32[16,128]{1,0:T(8,128)} custom-call(f32[4,6,2,2048]{3,2,1,0:T(2,128)} %bitcast.6, f32[4,3,2,2048]{3,2,1,0:T(2,128)} %bitcast.7, f32[4,2,2048]{2,1,0:T(2,128)} %rs_ref.1, f32[1,2048]{1,0:T(1,128)} %bitcast.9, s32[1,2048]{1,0:T(1,128)} %bitcast.10, s32[4,2048]{1,0:T(4,128)} %bitcast.8, f32[6,128]{1,0:T(8,128)} %dir_ref.1, f32[1,128]{1,0:T(1,128)} %bitcast.11), custom_call_target="tpu_custom_call" | custom-call | tf_op jit(solution)/shard_map/pallas_call | solution.py:426
  38.9 0.0 copy-done
  38.9 0.0 copy-done.1
  38.9 1.3 %slice_add_fusion = (f32[6,128]{1,0:T(8,128)}, f32[6,128]{1,0:T(8,128)}) fusion(f32[16,128]{1,0:T(8,128)} %shard_map.95, f32[6,128]{1,0:T(8,128)S(1)} %copy-done, f32[128]{0:T(128)S(1)} %copy-done.1), kind=kLoop, calls=%fused_computation | loop fusion | flops 1536 | bytes 15872 | tf_op jit(solution)/shard_map/add | solution.py:445
Async XLA Ops:
  0.6 38.3 %copy-start = (f32[6,128]{1,0:T(8,128)S(1)}, f32[6,128]{1,0:T(8,128)}, u32[]{:S(2)}) copy-start(f32[6,128]{1,0:T(8,128)} %dir_ref.1) | copy-start | bytes 9220
  0.6 38.3 %copy-start.1 = (f32[128]{0:T(128)S(1)}, f32[128]{0:T(128)}, u32[]{:S(2)}) copy-start(f32[128]{0:T(128)} %param.15) | copy-start | bytes 1540
